TPU v7x, 128 devices: a whole 4x4x4 slice. The times are simulated.
128 devices in a mesh: gx: 16 (over y, x), gy: 8 (over z, core).
Axes of the slice: x: 4, y: 4, z: 4, core: 2. Of those that a mesh axis runs over, the one named last changes fastest.
Arguments:
- tangent: float32 [32, 16, 256, 128], P('gx', 'gy')
- jacobians: float32 [32, 16, 2, 4, 256, 256], P('gx', 'gy')
- partner_codes: int32 [32, 16, 2, 4], P('gx', 'gy'), may hold values from 0 to 9, as said below
- owner_map: int32 [32, 16, 32], replicated, may hold values from 0 to 127, as said below
Outputs:
- q_owned: float32 [16384, 8, 128], P(('gx', 'gy'))
- r_factor: float32 [128, 128], replicated
Inputs may be any that keep to these rules, and one draw needn't show every extreme that they name: `partner_codes`: code c names the cell offset by c // 3 - 1 along the first dimension and c % 3 - 1 along the second; 9 marks an empty slot; slot 0 of every list is 4, the cell itself. `owner_map`: owners are numbered gx index times 8 plus gy index. Every owner receives exactly 128 blocks; each tile sends at most 2 blocks to one owner and exactly 2 to some owner; the counts a tile sends to the 128 owners are the same list for every tile up to order, and each owner receives each count of that list from exactly one tile.
All inputs are finite; a program needn't handle non-finite values.
Results may differ from a plain program's by a relative error of at most 0.0001.
Values sent between devices are 32-bit elements; how exact they have to be, the bound alone decides.
A program may use at most 64 MiB of HBM per device.

v0:
```python
import jax
import jax.numpy as jnp
from jax import lax
from jax.sharding import PartitionSpec as P

BR = 8


FULL_PRECISION = lax.Precision.HIGHEST


def extended_2(cells, sides, width):
    for axis, dim in sides:
        count = lax.axis_size(axis)
        head = lax.slice_in_dim(cells, 0, width, axis=dim)
        tail = lax.slice_in_dim(cells, cells.shape[dim] - width, cells.shape[dim], axis=dim)
        cells = jnp.concatenate(
            [
                lax.ppermute(tail, axis, [(i, (i + 1) % count) for i in range(count)]),
                cells,
                lax.ppermute(head, axis, [((i + 1) % count, i) for i in range(count)]),
            ],
            axis=dim,
        )
    return cells


def neighbour_terms(extended, jacobians_now, codes_now):
    cells_x = codes_now.shape[0]
    cells_y = codes_now.shape[1]
    codes_rest = codes_now[:, :, 1:]
    live_mask = (codes_rest != 9).astype(extended.dtype)
    codes_safe = jnp.where(codes_rest != 9, codes_rest, 4)
    index_x = jnp.arange(cells_x, dtype=jnp.int32)[:, None, None] + codes_safe // 3
    index_y = jnp.arange(cells_y, dtype=jnp.int32)[None, :, None] + codes_safe % 3
    flat_index = index_x * (cells_y + 2) + index_y
    cell_rows = extended.reshape((-1,) + extended.shape[2:])
    picked = cell_rows[flat_index] * live_mask[..., None, None]
    return jnp.einsum(
        "abkij,abkjv->abiv", jacobians_now[:, :, 1:], picked, precision=FULL_PRECISION
    )


def sweep_tile(field_now, jacobians_now, codes_now):
    own_term = jnp.einsum(
        "abij,abjv->abiv", jacobians_now[:, :, 0], field_now, precision=FULL_PRECISION
    )
    extended = extended_2(field_now, (("gx", 0), ("gy", 1)), 1)
    return own_term + neighbour_terms(extended, jacobians_now, codes_now)


def lower_cholesky(gram_mat):
    order = gram_mat.shape[0]
    places = jnp.arange(order, dtype=jnp.int32)

    def column_step(col_no, lower):
        row_now = lax.dynamic_index_in_dim(lower, col_no, 0, keepdims=False)
        row_now = jnp.where(places < col_no, row_now, 0.0)
        gram_col = lax.dynamic_index_in_dim(gram_mat, col_no, 1, keepdims=False)
        partial_sum = jnp.dot(lower, row_now, precision=FULL_PRECISION)
        pivot_sq = jnp.sum(jnp.where(places == col_no, gram_col - partial_sum, 0.0))
        pivot = jnp.sqrt(pivot_sq)
        column = (gram_col - partial_sum) / pivot
        column = jnp.where(places > col_no, column, jnp.where(places == col_no, pivot, 0.0))
        return lax.dynamic_update_slice(lower, column[:, None], (jnp.int32(0), col_no))

    return lax.fori_loop(0, order, column_step, jnp.zeros_like(gram_mat))


def lower_inverse(lower):
    order = lower.shape[0]
    places = jnp.arange(order, dtype=jnp.int32)

    def row_step(row_no, inverse):
        row_now = lax.dynamic_index_in_dim(lower, row_no, 0, keepdims=False)
        pivot = jnp.sum(jnp.where(places == row_no, row_now, 0.0))
        strict = jnp.where(places < row_no, row_now, 0.0)
        unit_row = (places == row_no).astype(lower.dtype)
        new_row = (unit_row - jnp.dot(strict, inverse, precision=FULL_PRECISION)) / pivot
        return lax.dynamic_update_slice(inverse, new_row[None, :], (row_no, jnp.int32(0)))

    return lax.fori_loop(0, order, row_step, jnp.zeros_like(lower))


def upper_factor(local_gram, rows_total):
    gram_sum = lax.psum(local_gram, ("gx", "gy"))
    lower = lower_cholesky(gram_sum / rows_total)
    return (lower.T, lower_inverse(lower))


def orthonormal(matrix, inverse_lower):
    return jnp.dot(matrix, inverse_lower.T, precision=FULL_PRECISION)


def pack_blocks(blocks, my_owners, tile_count, capacity):
    onehot = (my_owners[:, None] == jnp.arange(tile_count, dtype=jnp.int32)[None, :]).astype(
        jnp.int32
    )
    before = jnp.cumsum(onehot, axis=0) - onehot
    rank_in = jnp.sum(before * onehot, axis=1)
    slot_index = my_owners * capacity + rank_in
    buffer = jnp.zeros((tile_count * capacity,) + blocks.shape[1:], blocks.dtype)
    return buffer.at[slot_index].set(blocks)


def route_blocks(buffer, tiles_x, tiles_y, capacity):
    shaped = buffer.reshape((tiles_x * tiles_y, capacity) + buffer.shape[1:])
    arrived = lax.all_to_all(shaped, ("gx", "gy"), split_axis=0, concat_axis=0, tiled=True)
    return arrived.reshape((tiles_x * tiles_y * capacity,) + buffer.shape[1:])


def unpack_blocks(arrived, owner_map, my_tile, tiles_x, tiles_y, cells_x, cells_y, capacity):
    per_tile = owner_map.reshape(tiles_x, cells_x, tiles_y, cells_y, owner_map.shape[2])
    per_tile = per_tile.transpose(0, 2, 1, 3, 4).reshape(tiles_x * tiles_y, -1)
    counts = jnp.sum((per_tile == my_tile).astype(jnp.int32), axis=1)
    offsets = jnp.cumsum(counts) - counts
    target = jnp.arange(per_tile.shape[1], dtype=jnp.int32)
    source = jnp.sum((offsets[None, :] <= target[:, None]).astype(jnp.int32), axis=1) - 1
    position = source * capacity + target - offsets[source]
    return arrived[position]


def shards(tangent, jacobians, partner_codes, owner_map):
    cells_x, cells_y, rows_cell, vec_width = tangent.shape
    tiles_x = lax.axis_size("gx")
    tiles_y = lax.axis_size("gy")
    tile_count = tiles_x * tiles_y
    field_now = tangent
    for sweep_no in range(jacobians.shape[2]):
        field_now = sweep_tile(field_now, jacobians[:, :, sweep_no], partner_codes[:, :, sweep_no])
    matrix = field_now.reshape(-1, vec_width)
    block_count = matrix.shape[0] // BR
    capacity = 2 * block_count // tile_count
    tile_x = lax.axis_index("gx")
    tile_y = lax.axis_index("gy")
    my_tile = tile_x * tiles_y + tile_y
    my_owners = lax.dynamic_slice(
        owner_map, (tile_x * cells_x, tile_y * cells_y, 0), (cells_x, cells_y, owner_map.shape[2])
    ).reshape(-1)
    local_gram = jnp.dot(matrix.T, matrix, precision=FULL_PRECISION)
    rows_total = matrix.shape[0] * tile_count
    factor, inverse_lower = upper_factor(local_gram, rows_total)
    q_rows = orthonormal(matrix, inverse_lower)
    buffer = pack_blocks(
        q_rows.reshape(block_count, BR, vec_width), my_owners, tile_count, capacity
    )
    arrived = route_blocks(buffer, tiles_x, tiles_y, capacity)
    q_owned = unpack_blocks(
        arrived, owner_map, my_tile, tiles_x, tiles_y, cells_x, cells_y, capacity
    )
    return (q_owned, factor)


def solution(mesh):
    return jax.shard_map(
        shards,
        mesh=mesh,
        in_specs=(
            P("gx", "gy", None, None),
            P("gx", "gy", None, None, None, None),
            P("gx", "gy", None, None),
            P(),
        ),
        out_specs=(P(("gx", "gy"), None, None), P()),
        check_vma=False,
    )
```

profile of v0, /device:TPU:1, one launch (start us, length us, event | category | flops | bytes accessed | tf_op | source)
XLA Modules:
  0.0 712.4 jit_solution(8188136142010243980)
XLA Ops:
  7.2 1.1 fusion.59
  8.3 2.1 collective-permute-start
  10.4 3.8 collective-permute-start.1
  15.1 7.7 %fusion.55 = (f32[2,2,1,4,256,256]{5,4,3,2,1,0:T(8,128)}, f32[2,2,1,4,256,256]{5,4,3,2,1,0:T(8,128)}) fusion(f32[2,2,2,4,256,256]{5,4,3,2,1,0:T(8,128)} %param.9), kind=kLoop, calls=%fused_computation.99 | loop fusion | bytes 16777216 | tf_op jit(solution)/shard_map/slice | solution.py:130
  23.1 2.5 collective-permute-start.2
  25.7 6.1 copy_bitcast_fusion
  31.8 2.5 collective-permute-done.3
  34.5 1.9 gather_fusion
  36.4 1.9 copy.56
  38.3 4.8 fusion.31
  43.1 2.3 convolution_add_fusion.1
  45.5 4.8 collective-permute-start.5
  50.5 6.3 collective-permute-done.4
  58.4 4.8 collective-permute-done.6
  64.0 2.0 collective-permute-done.7
  66.0 1.4 pad_maximum_fusion.1
  67.4 1.8 gather_fusion.1
  69.2 1.9 copy.61
  71.1 5.2 fusion.36
  76.4 2.5 fusion.41
  78.8 1.2 convolution_bitcast_fusion.2
  80.3 139.4 %all-reduce.2.cloned.1.call-done = f32[128,128]{1,0:T(8,128)} async-done(((f32[128,128]{1,0:T(8,128)}), f32[128,128]{1,0:T(8,128)}) %all-reduce.2.cloned.1.call-update) | async-done | bytes 65552 | tf_op jit(solution)/shard_map/psum | solution.py:86
  219.7 0.8 broadcast_multiply_fusion
  220.7 258.7 %while.30 = (s32[]{:T(128)}, f32[128,128]{1,0:T(8,128)S(1)}, f32[128,128]{0,1:T(8,128)S(1)}, s32[]{:T(128)}, s32[]{:T(128)}) while((s32[]{:T(128)}, f32[128,128]{1,0:T(8,128)S(1)}, f32[128,128]{0,1:T(8,128)S(1)}, s32[]{:T(128)}, s32[]{:T(128)}) %tuple.82), condition=%wide.region_5.6_spmd.clone.clone, body=%wide.region_3.5_spmd.clone.clone.sunk | while | flops 198017 | bytes 72277 | solution.py:67
  220.7 0.8 fusion.78
  222.6 0.8 fusion.78
  224.6 0.8 fusion.78
  226.6 0.8 fusion.78
  228.7 0.8 fusion.78
  230.7 0.8 fusion.78
  232.7 0.8 fusion.78
  234.7 0.8 fusion.78
  236.8 0.8 fusion.78
  238.8 0.8 fusion.78
  240.8 0.8 fusion.78
  242.8 0.8 fusion.78
  244.8 0.8 fusion.78
  246.9 0.8 fusion.78
  248.9 0.8 fusion.78
  250.9 0.8 fusion.78
  252.9 0.8 fusion.78
  255.0 0.8 fusion.78
  257.0 0.8 fusion.78
  259.0 0.8 fusion.78
  261.0 0.8 fusion.78
  263.0 0.8 fusion.78
  265.1 0.8 fusion.78
  267.1 0.8 fusion.78
  269.1 0.8 fusion.78
  271.1 0.8 fusion.78
  273.2 0.8 fusion.78
  275.2 0.8 fusion.78
  277.2 0.8 fusion.78
  279.2 0.8 fusion.78
  281.2 0.8 fusion.78
  283.3 0.8 fusion.78
  285.3 0.8 fusion.78
  479.4 186.3 %while.31 = (s32[]{:T(128)}, f32[128,128]{1,0:T(8,128)S(1)}, f32[128,128]{1,0:T(8,128)S(1)}, s32[]{:T(128)}, s32[]{:T(128)}) while((s32[]{:T(128)}, f32[128,128]{1,0:T(8,128)S(1)}, f32[128,128]{1,0:T(8,128)S(1)}, s32[]{:T(128)}, s32[]{:T(128)}) %tuple.85), condition=%wide.region_8.9_spmd.clone.clone, body=%wide.region_6.8_spmd.clone.clone.sunk | while | flops 197761 | bytes 71237 | solution.py:82
  666.3 1.1 broadcast_in_dim.61
  667.3 12.4 %scatter_fusion = f32[256,8,128]{2,1,0:T(8,128)} fusion(f32[256,8,128]{2,1,0:T(8,128)} %broadcast_in_dim.61, s32[128]{0:T(128)S(1)} %fusion.51, f32[128,8,128]{2,1,0:T(8,128)S(1)} %fusion.44), kind=kCustom, calls=%fused_computation.4 | custom fusion | bytes 1573376 | tf_op jit(solution)/shard_map/scatter | solution.py:103
  679.7 5.1 all-to-all-start
  686.6 1.2 gather_fusion.2
  688.5 15.5 %all-to-all-done = f32[128,2,8,128]{3,2,1,0:T(8,128)S(1)} async-done(((f32[128,2,8,128]{3,2,1,0:T(8,128)}), f32[128,2,8,128]{3,2,1,0:T(8,128)S(1)}, u32[]{:S(2)}, u32[]{:S(2)}) %all-to-all-start) | async-done | bytes 1048608 | tf_op jit(solution)/shard_map/all_to_all | solution.py:108
  704.0 1.5 gather_fusion.3
  (926 shorter events, 330.0 us)
Async XLA Ops:
  7.2 212.5 %all-reduce.2.cloned.1.call-start = ((), (), s32[]{:S(2)}) async-start(), calls=%async_computation.1 | async-start | bytes 131072 | tf_op jit(solution)/shard_map/psum | solution.py:86
  8.3 14.7 %collective-permute-start = (f32[1,2,256,128]{3,2,1,0:T(8,128)S(1)}, f32[1,2,256,128]{3,2,1,0:T(8,128)S(1)}, u32[]{:S(2)}, u32[]{:S(2)}) collective-permute-start(f32[1,2,256,128]{3,2,1,0:T(8,128)S(1)} %get-tuple-element.249), channel_id=1, source_target_pairs={{0,8},{8,16},{16,24},{24,32},{32,40},{40,48},{48,56},{56,64},{64,7... | collective-permute-start | bytes 786440 | tf_op jit(solution)/shard_map/ppermute | solution.py:19
  10.4 12.6 %collective-permute-start.1 = (f32[1,2,256,128]{3,2,1,0:T(8,128)S(1)}, f32[1,2,256,128]{3,2,1,0:T(8,128)S(1)}, u32[]{:S(2)}, u32[]{:S(2)}) collective-permute-start(f32[1,2,256,128]{3,2,1,0:T(8,128)S(1)} %get-tuple-element.248), channel_id=1, source_target_pairs={{8,0},{16,8},{24,16},{32,24},{40,32},{48,40},{56,48},{64,56},{72,6... | collective-permute-start | bytes 786440 | tf_op jit(solution)/shard_map/ppermute | solution.py:21
  15.1 7.8 %copy-start.1 = (f32[2,2,256,128]{3,2,1,0:T(8,128)S(1)}, f32[2,2,256,128]{3,2,1,0:T(8,128)}, u32[]{:S(2)}) copy-start(f32[2,2,256,128]{3,2,1,0:T(8,128)} %param.8) | copy-start | bytes 1572868
  22.9 2.8 copy-start
  23.1 8.7 %collective-permute-start.2 = (f32[4,1,256,128]{3,2,1,0:T(8,128)S(1)}, f32[4,1,256,128]{3,2,1,0:T(8,128)S(1)}, u32[]{:S(2)}, u32[]{:S(2)}) collective-permute-start(f32[4,1,256,128]{3,2,1,0:T(8,128)S(1)} %get-tuple-element.244), channel_id=1, source_target_pairs={{0,1},{1,2},{2,3},{3,4},{4,5},{5,6},{6,7},{7,0},{8,9},{9,10},{10,1... | collective-permute-start | bytes 1572872 | tf_op jit(solution)/shard_map/ppermute | solution.py:19
  25.7 8.6 %collective-permute-start.3 = (f32[4,1,256,128]{3,2,1,0:T(8,128)S(1)}, f32[4,1,256,128]{3,2,1,0:T(8,128)S(1)}, u32[]{:S(2)}, u32[]{:S(2)}) collective-permute-start(f32[4,1,256,128]{3,2,1,0:T(8,128)S(1)} %get-tuple-element.245), channel_id=1, source_target_pairs={{1,0},{2,1},{3,2},{4,3},{5,4},{6,5},{7,6},{0,7},{9,8},{10,9},{11,1... | collective-permute-start | bytes 1572872 | tf_op jit(solution)/shard_map/ppermute | solution.py:21
  43.0 7.2 %copy-start.3 = (s32[32,16,32]{2,1,0:T(8,128)S(1)}, s32[32,16,32]{2,1,0:T(8,128)}, u32[]{:S(2)}) copy-start(s32[32,16,32]{2,1,0:T(8,128)} %param.11) | copy-start | bytes 196612
  45.4 11.4 %collective-permute-start.4 = (f32[1,2,256,128]{3,2,1,0:T(8,128)S(1)}, f32[1,2,256,128]{3,2,1,0:T(8,128)S(1)}, u32[]{:S(2)}, u32[]{:S(2)}) collective-permute-start(f32[1,2,256,128]{3,2,1,0:T(8,128)S(1)} %get-tuple-element.246), channel_id=1, source_target_pairs={{0,8},{8,16},{16,24},{24,32},{32,40},{40,48},{48,56},{56,64},{64,7... | collective-permute-start | bytes 786440 | tf_op jit(solution)/shard_map/ppermute | solution.py:19
  45.5 11.3 %collective-permute-start.5 = (f32[1,2,256,128]{3,2,1,0:T(8,128)S(1)}, f32[1,2,256,128]{3,2,1,0:T(8,128)S(1)}, u32[]{:S(2)}, u32[]{:S(2)}) collective-permute-start(f32[1,2,256,128]{3,2,1,0:T(8,128)S(1)} %get-tuple-element.247), channel_id=1, source_target_pairs={{8,0},{16,8},{24,16},{32,24},{40,32},{48,40},{56,48},{64,56},{72,6... | collective-permute-start | bytes 786440 | tf_op jit(solution)/shard_map/ppermute | solution.py:21
  57.0 6.3 collective-permute-start.6
  57.1 8.9 %collective-permute-start.7 = (f32[4,1,256,128]{3,2,1,0:T(8,128)S(1)}, f32[4,1,256,128]{3,2,1,0:T(8,128)}, u32[]{:S(2)}, u32[]{:S(2)}) collective-permute-start(f32[4,1,256,128]{3,2,1,0:T(8,128)S(1)} %get-tuple-element.243), channel_id=1, source_target_pairs={{1,0},{2,1},{3,2},{4,3},{5,4},{6,5},{7,6},{0,7},{9,8},{10,9},{11,1... | collective-permute-start | bytes 1572872 | tf_op jit(solution)/shard_map/ppermute | solution.py:21
  63.2 0.8 copy-start.2
  679.7 24.3 %all-to-all-start = ((f32[128,2,8,128]{3,2,1,0:T(8,128)}), f32[128,2,8,128]{3,2,1,0:T(8,128)S(1)}, u32[]{:S(2)}, u32[]{:S(2)}) async-start(f32[128,2,8,128]{3,2,1,0:T(8,128)} %bitcast.21), calls=%async_computation | async-start | bytes 2097152 | tf_op jit(solution)/shard_map/all_to_all | solution.py:108
Sparse Core Ops, SparseCore 0:
  80.2 139.4 all-reduce.1
where the time goes:
time: 716 us; the launch traced here: 712 us
  matrix products  224 us (31%)
  waiting for transfers between devices  171 us (24%)
  local copies, waits for them, and re-layouts  106 us (15%)
  loops' own time  95.3 us (13%)
  other arithmetic  82.9 us (12%)
  starting transfers between devices  19.2 us (3%)
  between operations  14.4 us (2%)
    psum x1, waiting for transfers between devices, upper_factor(): gram_sum = lax.psum(local_gram, ('gx', 'gy'))  139 us
    dot_general x128, matrix products, column_step(): partial_sum = jnp.dot(lower, row_now, precision=FULL_PRECISION)  105 us
    dot_general x128, matrix products, row_step(): jnp.dot(strict, inverse, precision=FULL_PRECISION)  102 us
    another operation x1, loops' own time, lower_cholesky(): return lax.fori_loop(0, order, column_step, jnp.zeros_like(gram_mat))  92.6 us
    reduce_sum x128, other arithmetic, row_step(): pivot = jnp.sum(jnp.where(places == row_no, row_now, 0.0))  77.6 us
    dynamic_update_slice x128, local copies, waits for them, and re-layouts, column_step(): lax.dynamic_update_slice(lower, column[:, None], (jnp.int32(0), col_no))  45.8 us
    all_to_all x1, waiting for transfers between devices, route_blocks(): lax.all_to_all(shaped, ('gx', 'gy'), split_axis=0, concat_axis=0, tiled=T...  15.5 us
    broadcast_in_dim x128, local copies, waits for them, and re-layouts, column_step(): column[:, None]  14.5 us
  transfers between devices with their start and end apart: 10, of which 6 were waited for; matrix products, arithmetic and copies ran while one was open for 3% of the time, Pallas kernels for 0%

commit v1 on v0

v1 whole, which is shorter than its diff:
```python
import jax
import jax.numpy as jnp
from jax import lax
from jax.experimental import pallas as pl
from jax.experimental.pallas import tpu as pltpu
from jax.sharding import PartitionSpec as P

F32 = jnp.float32
BF16 = jnp.bfloat16
I32 = jnp.int32
FULL = lax.Precision.HIGHEST
MESH = pl.DeviceIdType.MESH

GX, GY = 16, 8
TILES = GX * GY
ROWS = 131072
VEC = 128
CELL = 256
SWEEPS = 2
SLOTS = 4
BR = 8
BLK = 128


def dot(a, b, dims=((1,), (0,)), precision=None):
    return lax.dot_general(a, b, (dims, ((), ())), precision=precision, preferred_element_type=F32)


def split(x):
    high = x.astype(BF16)
    low = (x - high.astype(F32)).astype(BF16)
    return high, low


def iota(shape, dim):
    return lax.broadcasted_iota(I32, shape, dim)


def factor(work, r_out, inv_out):
    sub = iota((BR, VEC), 0)
    for blk in range(VEC // BR):
        lo = BR * blk
        left = work[lo : lo + BR, :VEC]
        right = work[lo : lo + BR, VEC:]
        for j in range(BR):
            k = lo + j
            col = jnp.broadcast_to(left[:, k : k + 1], (BR, VEC))
            pivot = jnp.broadcast_to(col[j : j + 1, :], (BR, VEC))
            inv = lax.rsqrt(pivot)
            inv = inv * (1.5 - 0.5 * (pivot * inv) * inv)
            coef = col * inv
            row_l = jnp.broadcast_to(left[j : j + 1, :], (BR, VEC)) * inv
            row_r = jnp.broadcast_to(right[j : j + 1, :], (BR, VEC)) * inv
            left = jnp.where(sub > j, left - coef * row_l, jnp.where(sub == j, row_l, left))
            right = jnp.where(sub > j, right - coef * row_r, jnp.where(sub == j, row_r, right))
        lane = iota((BR, VEC), 1)
        r_out[lo : lo + BR, :] = jnp.where(lane >= sub + lo, left, 0.0)
        inv_out[lo : lo + BR, :] = right
        if lo + BR < VEC:
            both = jnp.concatenate([left, right], axis=1)
            update = dot(left, both, ((0,), (0,)), FULL)
            work[lo + BR :, :] = work[lo + BR :, :] - update[lo + BR :, :]


def kernel(
    tan, jac, codes, owners, q_out, r_out,
    jv, jhi, jlo, ext0, ext1, acc, amat, omv, idxv, idxs,
    gram, rsb, part, gxb, tot, gfull, work, linv, pk, arr,
    loc_sem, jac_sem, hsend, hrecv, ar_send, ar_recv, a2a_send, a2a_recv, idx_sem,
):
    gx = lax.axis_index("gx")
    gy = lax.axis_index("gy")
    me = gx * GY + gy
    core = lax.rem(gy, 2)
    off, on = core, 1 - core
    gx_hi, gx_lo = lax.rem(gx + 1, GX), lax.rem(gx + GX - 1, GX)
    gy_off = lax.rem(gy + 2 * core - 1 + GY, GY)
    gy_on = lax.rem(gy + 1 - 2 * core + GY, GY)

    def halo(s, src, dst, who, role):
        return pltpu.make_async_remote_copy(
            src_ref=src, dst_ref=dst, send_sem=hsend.at[s, role], recv_sem=hrecv.at[s, role],
            device_id=who, device_id_type=MESH,
        )

    def own(s, ext, a, b):
        return tan.at[a * 2 + b] if s == 0 else ext.at[(1 + a) * 4 + 1 + b]

    def own_copies(s, ext):
        cols = (off, on)
        x_copies = [
            (
                halo(s, own(s, ext, 1, cols[k]), ext.at[1 + cols[k]], (gx_hi, gy), k),
                halo(s, own(s, ext, 0, cols[k]), ext.at[12 + 1 + cols[k]], (gx_lo, gy), 2 + k),
            )
            for k in range(2)
        ]
        y_off = [
            halo(s, own(s, ext, a, off), ext.at[(1 + a) * 4 + 3 * on], (gx, gy_off), 4 + a)
            for a in range(2)
        ]
        y_on = [
            halo(s, own(s, ext, a, on), ext.at[(1 + a) * 4 + 3 * off], (gx, gy_on), 6 + a)
            for a in range(2)
        ]
        return x_copies, y_off, y_on

    def corner_copies(s, ext):
        c_off = [
            halo(s, ext.at[12 * side + 1 + off], ext.at[12 * side + 3 * on], (gx, gy_off), 8 + side)
            for side in range(2)
        ]
        c_on = [
            halo(s, ext.at[12 * side + 1 + on], ext.at[12 * side + 3 * off], (gx, gy_on), 10 + side)
            for side in range(2)
        ]
        return c_off, c_on

    exts = (ext0, ext1)
    sent = []

    x_c, y_off, y_on = own_copies(0, ext0)
    for copy in (*x_c[0], *y_off, *x_c[1], *y_on):
        copy.start()
    locals_ = [
        pltpu.make_async_copy(tan.at[c], ext0.at[(1 + c // 2) * 4 + 1 + c % 2], loc_sem.at[c])
        for c in range(4)
    ]
    for copy in locals_:
        copy.start()
    own_copy = pltpu.make_async_copy(owners, omv, loc_sem.at[4])
    own_copy.start()
    jac_copies = [
        pltpu.make_async_copy(jac.at[:, s], jv.at[s], jac_sem.at[s]) for s in range(SWEEPS)
    ]
    for copy in jac_copies:
        copy.start()

    def product(s, cell, slot, field):
        high, low = split(field)
        j_high = jhi[s, cell, slot]
        j_low = jlo[s, cell, slot]
        wide = dot(j_high, jnp.concatenate([high, low], axis=1))
        return wide[:, :VEC] + (wide[:, VEC:] + dot(j_low, high))

    def split_jacobians(s):
        def body(n, carry):
            cell, slot = lax.div(n, SLOTS), lax.rem(n, SLOTS)
            high, low = split(jv[s, cell, slot])
            jhi[s, cell, slot] = high
            jlo[s, cell, slot] = low
            return carry

        lax.fori_loop(0, 4 * SLOTS, body, 0)

    def own_terms(s, ext):
        def body(cell, carry):
            at = (1 + lax.div(cell, 2)) * 4 + 1 + lax.rem(cell, 2)
            acc[cell] = product(s, cell, 0, ext[at])
            return carry

        lax.fori_loop(0, 4, body, 0)

    def routing():
        ones = jnp.ones((32, VEC), BF16)
        mine = (omv[...] == me).astype(F32).astype(BF16)
        per_cell = dot(mine, ones).astype(BF16)
        cell = iota((TILES, 512), 1)
        tile_of = lax.shift_right_logical(cell, 5) * 8 + lax.shift_right_logical(cell & 15, 1)
        pick = (tile_of == iota((TILES, 512), 0)).astype(F32).astype(BF16)
        count = dot(pick, per_cell)
        rows, lanes = iota((TILES, TILES), 0), iota((TILES, TILES), 1)
        tri = (lanes <= rows).astype(F32).astype(BF16)
        ends = dot(tri, count.astype(BF16))
        places = lanes.astype(F32)
        before = (ends <= places).astype(F32)
        tile_at = jnp.sum(before, axis=0, keepdims=True)
        passed = jnp.sum(before * count, axis=0, keepdims=True)
        slot_at = jnp.clip(2.0 * tile_at + places[:1] - passed, 0.0, 2.0 * TILES - 1.0)
        diag = iota((32, 32), 0) == iota((32, 32), 1)
        stack = []
        for c in range(4):
            row = omv[pl.ds((2 * gx + c // 2) * 16 + 2 * gy + c % 2, 1), :].astype(F32)
            stack.append(jnp.where(diag, jnp.broadcast_to(row, (32, 32)), 0.0))
        owner_of = dot(jnp.concatenate(stack, axis=0).astype(BF16), ones)
        hit = owner_of == places
        order = rows.astype(F32)
        first = jnp.min(jnp.where(hit, order, float(BLK - 1)), axis=0, keepdims=True)
        last = jnp.max(jnp.where(hit, order, 0.0), axis=0, keepdims=True)
        table = jnp.concatenate([first, last, slot_at, jnp.zeros((5, VEC), F32)], axis=0)
        idxv[...] = table.astype(I32)
        copy = pltpu.make_async_copy(idxv, idxs, idx_sem)
        copy.start()
        return copy

    idx_copy = None
    for s in range(SWEEPS):
        ext = exts[s]
        sent += [*x_c[0], *x_c[1], *y_off, *y_on]
        if s == 0:
            jac_copies[0].wait()
            split_jacobians(0)
            for copy in locals_:
                copy.wait()
        own_terms(s, ext)
        c_off, c_on = corner_copies(s, ext)
        for copy in x_c[0]:
            copy.wait_recv()
        for copy in c_off:
            copy.start()
        for copy in x_c[1]:
            copy.wait_recv()
        for copy in c_on:
            copy.start()
        sent += [*c_off, *c_on]
        if s == 0:
            jac_copies[1].wait()
            split_jacobians(1)
            own_copy.wait()
            idx_copy = routing()
        for copy in (*y_on, *y_off, *c_on, *c_off):
            copy.wait_recv()

        if s == 0:
            x_c, y_off, y_on = own_copies(1, ext1)
        for n in range(4):
            a, b = n % 2, (off if n < 2 else on)
            cell = a * 2 + b
            total = acc[cell]
            for slot in range(1, SLOTS):
                code = codes[(cell * SWEEPS + s) * SLOTS + slot]
                live = jnp.where(code != 9, 1.0, 0.0).astype(F32)
                safe = jnp.where(code != 9, code, 4)
                step_x = lax.shift_right_logical(safe * 11, 5)
                step_y = safe - 3 * step_x
                field = ext[(a + step_x) * 4 + b + step_y] * live
                total = total + product(s, cell, slot, field)
            if s == 0:
                ext1[(1 + a) * 4 + 1 + b] = total
                if n == 1:
                    for copy in (*x_c[0], *y_off):
                        copy.start()
                if n == 3:
                    for copy in (*x_c[1], *y_on):
                        copy.start()
            else:
                amat[pl.ds(cell * 32, 32)] = total.reshape(32, BR, VEC)

    rows_all = amat[...].reshape(4 * CELL, VEC)
    gram[...] = dot(rows_all, rows_all, ((0,), (0,)), FULL)
    share = VEC // GY

    def to_gy(step, src, dst, phase):
        k = lax.rem(gy + step, GY)
        return pltpu.make_async_remote_copy(
            src_ref=src(k), dst_ref=dst, send_sem=ar_send.at[phase], recv_sem=ar_recv.at[phase],
            device_id=(gx, k), device_id_type=MESH,
        )

    def wait_bytes(ref, sem):
        pltpu.make_async_copy(ref, ref, sem).wait()

    for step in range(1, GY):
        to_gy(step, lambda k: gram.at[pl.ds(k * share, share)], rsb.at[gy], 0).start()
    rsb[gy] = gram[pl.ds(gy * share, share), :]

    idx_copy.wait()

    def pack(o, carry):
        pk[o, 0] = amat[idxs[0, o] & (BLK - 1)]
        pk[o, 1] = amat[idxs[1, o] & (BLK - 1)]
        return carry

    lax.fori_loop(0, TILES // 2, pack, 0, unroll=8)
    wait_bytes(rsb.at[pl.ds(0, GY - 1)], ar_recv.at[0])
    mine = jnp.sum(rsb[...], axis=0)
    part[...] = mine
    for step in range(1, GX):
        pltpu.make_async_remote_copy(
            src_ref=part, dst_ref=gxb.at[gx], send_sem=ar_send.at[1], recv_sem=ar_recv.at[1],
            device_id=(lax.rem(gx + step, GX), gy), device_id_type=MESH,
        ).start()
    gxb[gx] = mine
    lax.fori_loop(TILES // 2, TILES, pack, 0, unroll=8)
    wait_bytes(gxb.at[pl.ds(0, GX - 1)], ar_recv.at[1])
    mine = jnp.sum(gxb[...], axis=0) * (1.0 / ROWS)
    tot[...] = mine
    for step in range(1, GY):
        to_gy(step, lambda k: tot, gfull.at[pl.ds(gy * share, share)], 2).start()
    gfull[pl.ds(gy * share, share), :] = mine
    wait_bytes(gfull.at[pl.ds(0, (GY - 1) * share)], ar_recv.at[2])

    def send(step, carry):
        o = lax.rem(me + step, TILES)
        pltpu.make_async_remote_copy(
            src_ref=pk.at[o], dst_ref=arr.at[me], send_sem=a2a_send, recv_sem=a2a_recv,
            device_id=(lax.div(o, GY), lax.rem(o, GY)), device_id_type=MESH,
        ).start()
        return carry

    lax.fori_loop(1, TILES, send, 0)
    arr[me] = pk[me]

    eye = (iota((VEC, VEC), 0) == iota((VEC, VEC), 1)).astype(F32)
    work[:, :VEC] = gfull[...]
    work[:, VEC:] = eye
    factor(work, r_out, linv)

    wait_bytes(arr.at[pl.ds(0, TILES - 1)], a2a_recv)

    def unpack(p, carry):
        at = idxs[2, p] & (2 * TILES - 1)
        amat[p] = arr[lax.shift_right_logical(at, 1), at & 1]
        return carry

    lax.fori_loop(0, BLK, unpack, 0, unroll=8)
    rows_all = amat[...].reshape(4 * CELL, VEC)
    q_out[...] = dot(rows_all, linv[...], ((1,), (1,)), FULL).reshape(BLK, BR, VEC)

    for copy in sent:
        copy.wait_send()
    wait_bytes(rsb.at[pl.ds(0, GY - 1)], ar_send.at[0])
    wait_bytes(gxb.at[pl.ds(0, GX - 1)], ar_send.at[1])
    wait_bytes(gfull.at[pl.ds(0, (GY - 1) * share)], ar_send.at[2])
    wait_bytes(arr.at[pl.ds(0, TILES - 1)], a2a_send)


def shards(tangent, jacobians, partner_codes, owner_map):
    hbm = pl.BlockSpec(memory_space=pl.ANY)
    vmem = pl.BlockSpec(memory_space=pltpu.VMEM)
    cells = (4, CELL, VEC)
    return pl.pallas_call(
        kernel,
        out_shape=(
            jax.ShapeDtypeStruct((BLK, BR, VEC), F32),
            jax.ShapeDtypeStruct((VEC, VEC), F32),
        ),
        in_specs=[hbm, hbm, pl.BlockSpec(memory_space=pltpu.SMEM), hbm],
        out_specs=(vmem, vmem),
        scratch_shapes=[
            pltpu.VMEM((SWEEPS, 4, SLOTS, CELL, CELL), F32),
            pltpu.VMEM((SWEEPS, 4, SLOTS, CELL, CELL), BF16),
            pltpu.VMEM((SWEEPS, 4, SLOTS, CELL, CELL), BF16),
            pltpu.VMEM((16, CELL, VEC), F32),
            pltpu.VMEM((16, CELL, VEC), F32),
            pltpu.VMEM(cells, F32),
            pltpu.VMEM((BLK, BR, VEC), F32),
            pltpu.VMEM((512, 32), I32),
            pltpu.VMEM((8, VEC), I32),
            pltpu.SMEM((8, VEC), I32),
            pltpu.VMEM((VEC, VEC), F32),
            pltpu.VMEM((GY, VEC // GY, VEC), F32),
            pltpu.VMEM((VEC // GY, VEC), F32),
            pltpu.VMEM((GX, VEC // GY, VEC), F32),
            pltpu.VMEM((VEC // GY, VEC), F32),
            pltpu.VMEM((VEC, VEC), F32),
            pltpu.VMEM((VEC, 2 * VEC), F32),
            pltpu.VMEM((VEC, VEC), F32),
            pltpu.VMEM((TILES, 2, BR, VEC), F32),
            pltpu.VMEM((TILES, 2, BR, VEC), F32),
            pltpu.SemaphoreType.DMA((5,)),
            pltpu.SemaphoreType.DMA((SWEEPS,)),
            pltpu.SemaphoreType.DMA((SWEEPS, 12)),
            pltpu.SemaphoreType.DMA((SWEEPS, 12)),
            pltpu.SemaphoreType.DMA((3,)),
            pltpu.SemaphoreType.DMA((3,)),
            pltpu.SemaphoreType.DMA,
            pltpu.SemaphoreType.DMA,
            pltpu.SemaphoreType.DMA,
        ],
        compiler_params=pltpu.CompilerParams(
            has_side_effects=True, vmem_limit_bytes=52 * 2**20
        ),
    )(
        tangent.reshape(cells),
        jacobians.reshape(4, SWEEPS, SLOTS, CELL, CELL),
        partner_codes.reshape(-1),
        owner_map.reshape(-1, owner_map.shape[2]),
    )


def solution(mesh):
    return jax.shard_map(
        shards,
        mesh=mesh,
        in_specs=(
            P("gx", "gy", None, None),
            P("gx", "gy", None, None, None, None),
            P("gx", "gy", None, None),
            P(),
        ),
        out_specs=(P(("gx", "gy"), None, None), P()),
        check_vma=False,
    )
```

time: 716 us -> 81.1 us (0.11)
  matrix products: 224 us -> 0 us
  waiting for transfers between devices: 171 us -> 0 us
  local copies, waits for them, and re-layouts: 106 us -> 4.19 us
  loops' own time: 95.3 us -> 0 us
  other arithmetic: 82.9 us -> 0 us
  Pallas kernels: 0 us -> 76.1 us
  starting transfers between devices: 19.2 us -> 0 us
  between operations: 14.4 us -> 0.64 us
    dot_general x262 -> x0, matrix products: 224 us -> none  [the longest x128 105 us: column_step(): partial_sum = jnp.dot(lower, row_now, precision=FULL_PRECISION)]
    psum x1 -> x0, waiting for transfers between devices: 139 us -> none  [upper_factor(): gram_sum = lax.psum(local_gram, ('gx', 'gy'))]
    another operation x2 -> x0, loops' own time: 95.3 us -> none  [the longest x1 92.6 us: lower_cholesky(): return lax.fori_loop(0, order, column_step, jnp.zeros_like(gram_mat))]
    reduce_sum x132 -> x0, other arithmetic: 78.7 us -> none  [the longest x128 77.6 us: row_step(): pivot = jnp.sum(jnp.where(places == row_no, row_now, 0.0))]
    pallas_call x0 -> x1, Pallas kernels: none -> 76.1 us  [shards(): pl.pallas_call(kernel, out_shape=(jax.ShapeDtypeStruct((BLK, BR, VEC), F3...]
    dynamic_update_slice x256 -> x0, local copies, waits for them, and re-layouts: 49.8 us -> none  [the longest x128 45.8 us: column_step(): lax.dynamic_update_slice(lower, column[:, None], (jnp.int32(0), col_no))]
    broadcast_in_dim x131 -> x0, local copies, waits for them, and re-layouts: 15.7 us -> none  [the longest x128 14.5 us: column_step(): column[:, None]]
    ppermute x8 -> x0, waiting for transfers between devices: 15.6 us -> none  [the longest x4 11.1 us: extended_2(): lax.ppermute(tail, axis, [(i, (i + 1) % count) for i in range(count)])]
  transfers between devices with their start and end apart: 10 -> 0, of which waited for: 6 -> 0; matrix products, arithmetic and copies ran while one was open for 3% -> 0% of each run, Pallas kernels for 0% -> 0%
where the time goes in v1:
time: 81.1 us; the launch traced here: 80.9 us
  Pallas kernels  76.1 us (94%)
  local copies, waits for them, and re-layouts  4.19 us (5%)
    pallas_call x1, Pallas kernels, shards(): pl.pallas_call(kernel, out_shape=(jax.ShapeDtypeStruct((BLK, BR, VEC), F3...  76.1 us
    unnamed x6, local copies, waits for them, and re-layouts  3.42 us

profile of v1, /device:TPU:1, one launch (start us, length us, event | category | flops | bytes accessed | tf_op | source)
XLA Modules:
  0.0 80.9 jit_solution(17802134786434766716)
XLA Ops:
  0.6 0.8 reshape.18.codes
  1.4 0.0 copy-start
  1.4 1.0 %copy-done = f32[2,2,256,128]{3,2,1,0:T(8,128)S(1)} copy-done((f32[2,2,256,128]{3,2,1,0:T(8,128)S(1)}, f32[2,2,256,128]{3,2,1,0:T(8,128)}, u32[]{:S(2)}) %copy-start) | copy-done | bytes 524312
  2.4 0.0 copy-start.1
  2.4 0.9 %copy-done.1 = s32[32,16,32]{2,1,0:T(8,128)S(1)} copy-done((s32[32,16,32]{2,1,0:T(8,128)S(1)}, s32[32,16,32]{2,1,0:T(8,128)}, u32[]{:S(2)}) %copy-start.1) | copy-done | bytes 65560
  3.4 76.1 %shard_map.59 = (f32[128,8,128]{2,1,0:T(8,128)S(1)}, f32[128,128]{1,0:T(8,128)S(1)}) custom-call(f32[4,256,128]{2,1,0:T(8,128)S(1)} %bitcast.3, f32[4,2,4,256,256]{4,3,2,1,0:T(8,128)} %bitcast.5, s32[32]{0:T(128)S(1)} %reshape.18.codes, s32[512,32]{1,0:T(8,128)S(1)} %bitcast.4), custom_call_target="tpu_custom_call" | custom-call | tf_op jit(solution)/shard_map/pallas_call | solution.py:332
  79.5 0.8 copy.8
  80.3 0.6 copy.9
Async XLA Ops:
  1.4 1.0 %copy-start = (f32[2,2,256,128]{3,2,1,0:T(8,128)S(1)}, f32[2,2,256,128]{3,2,1,0:T(8,128)}, u32[]{:S(2)}) copy-start(f32[2,2,256,128]{3,2,1,0:T(8,128)} %param.4) | copy-start | bytes 1572868
  2.4 0.9 %copy-start.1 = (s32[32,16,32]{2,1,0:T(8,128)S(1)}, s32[32,16,32]{2,1,0:T(8,128)}, u32[]{:S(2)}) copy-start(s32[32,16,32]{2,1,0:T(8,128)} %param.7) | copy-start | bytes 196612

commit v2 on v1

--- a/solution.py
+++ b/solution.py
@@ -36,30 +36,62 @@
     return lax.broadcasted_iota(I32, shape, dim)
 
 
+def spread(x):
+    return jnp.broadcast_to(x, (BR, VEC))
+
+
+def thirds(x):
+    high = x.astype(BF16).astype(F32)
+    rest = x - high
+    mid = rest.astype(BF16).astype(F32)
+    low = (rest - mid).astype(BF16).astype(F32)
+    return high, mid, low
+
+
+def outer(left, both):
+    h, m, l = thirds(left)
+    hh, mm, ll = thirds(both)
+    a = jnp.concatenate([h, h, m, h, m, l], axis=0).astype(BF16)
+    b = jnp.concatenate([hh, mm, hh, ll, mm, hh], axis=0).astype(BF16)
+    return dot(a, b, ((0,), (0,)))
+
+
+def panel(left, right, lo):
+    sub = iota((BR, VEC), 0)
+    cols = [spread(left[:, lo + j : lo + j + 1]) for j in range(BR)]
+    block = [[spread(cols[j][i : i + 1, :]) for j in range(i + 1)] for i in range(BR)]
+    rows_l = [spread(left[i : i + 1, :]) for i in range(BR)]
+    rows_r = [spread(right[i : i + 1, :]) for i in range(BR)]
+    for j in range(BR):
+        pivot = block[j][j]
+        inv = lax.rsqrt(pivot)
+        inv = inv * (1.5 - 0.5 * (pivot * inv) * inv)
+        rows_l[j] = rows_l[j] * inv
+        rows_r[j] = rows_r[j] * inv
+        below = [block[i][j] * inv if i > j else None for i in range(BR)]
+        for i in range(j + 1, BR):
+            for k in range(j + 1, i + 1):
+                block[i][k] = block[i][k] - below[i] * below[k]
+        for i in range(j + 1, BR):
+            rows_l[i] = rows_l[i] - below[i] * rows_l[j]
+            rows_r[i] = rows_r[i] - below[i] * rows_r[j]
+    left, right = rows_l[0], rows_r[0]
+    for j in range(1, BR):
+        left = jnp.where(sub == j, rows_l[j], left)
+        right = jnp.where(sub == j, rows_r[j], right)
+    return left, right
+
+
 def factor(work, r_out, inv_out):
-    sub = iota((BR, VEC), 0)
-    for blk in range(VEC // BR):
-        lo = BR * blk
-        left = work[lo : lo + BR, :VEC]
-        right = work[lo : lo + BR, VEC:]
-        for j in range(BR):
-            k = lo + j
-            col = jnp.broadcast_to(left[:, k : k + 1], (BR, VEC))
-            pivot = jnp.broadcast_to(col[j : j + 1, :], (BR, VEC))
-            inv = lax.rsqrt(pivot)
-            inv = inv * (1.5 - 0.5 * (pivot * inv) * inv)
-            coef = col * inv
-            row_l = jnp.broadcast_to(left[j : j + 1, :], (BR, VEC)) * inv
-            row_r = jnp.broadcast_to(right[j : j + 1, :], (BR, VEC)) * inv
-            left = jnp.where(sub > j, left - coef * row_l, jnp.where(sub == j, row_l, left))
-            right = jnp.where(sub > j, right - coef * row_r, jnp.where(sub == j, row_r, right))
-        lane = iota((BR, VEC), 1)
-        r_out[lo : lo + BR, :] = jnp.where(lane >= sub + lo, left, 0.0)
-        inv_out[lo : lo + BR, :] = right
-        if lo + BR < VEC:
-            both = jnp.concatenate([left, right], axis=1)
-            update = dot(left, both, ((0,), (0,)), FULL)
-            work[lo + BR :, :] = work[lo + BR :, :] - update[lo + BR :, :]
+    sub, lane = iota((BR, VEC), 0), iota((BR, VEC), 1)
+    for lo in range(0, VEC, BR):
+        hi = lo + BR
+        left, right = panel(work[lo:hi, :VEC], work[lo:hi, VEC:], lo)
+        r_out[lo:hi, :] = jnp.where(lane >= sub + lo, left, 0.0)
+        inv_out[lo:hi, :] = right
+        if hi < VEC:
+            update = outer(left, jnp.concatenate([left, right], axis=1))
+            work[hi:, :] = work[hi:, :] - update[hi:, :]
 
 
 def kernel(
@@ -67,6 +99,7 @@
     jv, jhi, jlo, ext0, ext1, acc, amat, omv, idxv, idxs,
     gram, rsb, part, gxb, tot, gfull, work, linv, pk, arr,
     loc_sem, jac_sem, hsend, hrecv, ar_send, ar_recv, a2a_send, a2a_recv, idx_sem,
+    far_x, farther_x, far_y,
 ):
     gx = lax.axis_index("gx")
     gy = lax.axis_index("gy")
@@ -119,21 +152,32 @@
     exts = (ext0, ext1)
     sent = []
 
-    x_c, y_off, y_on = own_copies(0, ext0)
-    for copy in (*x_c[0], *y_off, *x_c[1], *y_on):
-        copy.start()
+    def along_x(step):
+        return (lax.rem(gx + step + GX, GX), gy)
+
+    def along_y(step):
+        return (gx, lax.rem(gy + step + GY, GY))
+
+    def greet(sem, who):
+        for device in who:
+            pl.semaphore_signal(sem, inc=1, device_id=device, device_id_type=MESH)
+
+    barrier = pltpu.get_barrier_semaphore()
+    greet(barrier, (along_x(1), along_x(-1), along_y(1), along_y(-1)))
     locals_ = [
         pltpu.make_async_copy(tan.at[c], ext0.at[(1 + c // 2) * 4 + 1 + c % 2], loc_sem.at[c])
         for c in range(4)
     ]
-    for copy in locals_:
-        copy.start()
     own_copy = pltpu.make_async_copy(owners, omv, loc_sem.at[4])
-    own_copy.start()
     jac_copies = [
         pltpu.make_async_copy(jac.at[:, s], jv.at[s], jac_sem.at[s]) for s in range(SWEEPS)
     ]
-    for copy in jac_copies:
+    for copy in (*locals_, own_copy, *jac_copies):
+        copy.start()
+    pl.semaphore_wait(barrier, 4)
+
+    x_c, y_off, y_on = own_copies(0, ext0)
+    for copy in (*x_c[0], *y_off, *x_c[1], *y_on):
         copy.start()
 
     def product(s, cell, slot, field):
@@ -212,6 +256,10 @@
             copy.wait_recv()
         for copy in c_on:
             copy.start()
+        if s == 0:
+            greet(far_x, (along_x(2), along_x(-2)))
+        else:
+            pl.semaphore_wait(farther_x, 2)
         sent += [*c_off, *c_on]
         if s == 0:
             jac_copies[1].wait()
@@ -220,6 +268,12 @@
             idx_copy = routing()
         for copy in (*y_on, *y_off, *c_on, *c_off):
             copy.wait_recv()
+        if s == 0:
+            pl.semaphore_wait(far_x, 2)
+            greet(farther_x, (along_x(4), along_x(-4)))
+            greet(far_y, (along_y(2), along_y(-2)))
+        else:
+            pl.semaphore_wait(far_y, 2)
 
         if s == 0:
             x_c, y_off, y_on = own_copies(1, ext1)
@@ -228,7 +282,7 @@
             cell = a * 2 + b
             total = acc[cell]
             for slot in range(1, SLOTS):
-                code = codes[(cell * SWEEPS + s) * SLOTS + slot]
+                code = codes[a, b, s, slot]
                 live = jnp.where(code != 9, 1.0, 0.0).astype(F32)
                 safe = jnp.where(code != 9, code, 4)
                 step_x = lax.shift_right_logical(safe * 11, 5)
@@ -271,7 +325,16 @@
         pk[o, 1] = amat[idxs[1, o] & (BLK - 1)]
         return carry
 
-    lax.fori_loop(0, TILES // 2, pack, 0, unroll=8)
+    def send(step, carry):
+        o = lax.rem(me + 37 * step, TILES)
+        pltpu.make_async_remote_copy(
+            src_ref=pk.at[o], dst_ref=arr.at[me], send_sem=a2a_send, recv_sem=a2a_recv,
+            device_id=(lax.div(o, GY), lax.rem(o, GY)), device_id_type=MESH,
+        ).start()
+        return carry
+
+    lax.fori_loop(0, TILES, pack, 0, unroll=8)
+    arr[me] = pk[me]
     wait_bytes(rsb.at[pl.ds(0, GY - 1)], ar_recv.at[0])
     mine = jnp.sum(rsb[...], axis=0)
     part[...] = mine
@@ -281,25 +344,16 @@
             device_id=(lax.rem(gx + step, GX), gy), device_id_type=MESH,
         ).start()
     gxb[gx] = mine
-    lax.fori_loop(TILES // 2, TILES, pack, 0, unroll=8)
+    lax.fori_loop(1, 49, send, 0)
     wait_bytes(gxb.at[pl.ds(0, GX - 1)], ar_recv.at[1])
     mine = jnp.sum(gxb[...], axis=0) * (1.0 / ROWS)
     tot[...] = mine
     for step in range(1, GY):
         to_gy(step, lambda k: tot, gfull.at[pl.ds(gy * share, share)], 2).start()
     gfull[pl.ds(gy * share, share), :] = mine
+    lax.fori_loop(49, 97, send, 0)
     wait_bytes(gfull.at[pl.ds(0, (GY - 1) * share)], ar_recv.at[2])
-
-    def send(step, carry):
-        o = lax.rem(me + step, TILES)
-        pltpu.make_async_remote_copy(
-            src_ref=pk.at[o], dst_ref=arr.at[me], send_sem=a2a_send, recv_sem=a2a_recv,
-            device_id=(lax.div(o, GY), lax.rem(o, GY)), device_id_type=MESH,
-        ).start()
-        return carry
-
-    lax.fori_loop(1, TILES, send, 0)
-    arr[me] = pk[me]
+    lax.fori_loop(97, TILES, send, 0)
 
     eye = (iota((VEC, VEC), 0) == iota((VEC, VEC), 1)).astype(F32)
     work[:, :VEC] = gfull[...]
@@ -326,7 +380,7 @@
 
 
 def shards(tangent, jacobians, partner_codes, owner_map):
-    hbm = pl.BlockSpec(memory_space=pl.ANY)
+    hbm = pl.BlockSpec(memory_space=pltpu.HBM)
     vmem = pl.BlockSpec(memory_space=pltpu.VMEM)
     cells = (4, CELL, VEC)
     return pl.pallas_call(
@@ -367,14 +421,17 @@
             pltpu.SemaphoreType.DMA,
             pltpu.SemaphoreType.DMA,
             pltpu.SemaphoreType.DMA,
+            pltpu.SemaphoreType.REGULAR,
+            pltpu.SemaphoreType.REGULAR,
+            pltpu.SemaphoreType.REGULAR,
         ],
         compiler_params=pltpu.CompilerParams(
-            has_side_effects=True, vmem_limit_bytes=52 * 2**20
+            collective_id=0, has_side_effects=True, vmem_limit_bytes=62 * 2**20
         ),
     )(
         tangent.reshape(cells),
         jacobians.reshape(4, SWEEPS, SLOTS, CELL, CELL),
-        partner_codes.reshape(-1),
+        partner_codes,
         owner_map.reshape(-1, owner_map.shape[2]),
     )
 

time: 81.1 us -> 63.2 us (0.78)
  Pallas kernels: 76.1 us -> 59 us
  local copies, waits for them, and re-layouts: 4.19 us -> 3.34 us
    pallas_call x1, Pallas kernels: 76.1 us -> 59 us  [shards(): pl.pallas_call(kernel, out_shape=(jax.ShapeDtypeStruct((BLK, BR, VEC), F3...]
    unnamed x6 -> x2, local copies, waits for them, and re-layouts: 3.42 us -> 3.34 us
where the time goes in v2:
time: 63.2 us; the launch traced here: 63 us
  Pallas kernels  59 us (93%)
  local copies, waits for them, and re-layouts  3.34 us (5%)
  between operations  0.64 us (1%)
    pallas_call x1, Pallas kernels, shards(): pl.pallas_call(kernel, out_shape=(jax.ShapeDtypeStruct((BLK, BR, VEC), F3...  59 us
    unnamed x2, local copies, waits for them, and re-layouts  3.34 us

profile of v2, /device:TPU:1, one launch (start us, length us, event | category | flops | bytes accessed | tf_op | source)
XLA Modules:
  0.0 63.0 jit_solution(10646446281779390328)
XLA Ops:
  0.6 59.0 %shard_map.59 = (f32[128,8,128]{2,1,0:T(8,128)}, f32[128,128]{1,0:T(8,128)}) custom-call(f32[4,256,128]{2,1,0:T(8,128)} %bitcast.4, f32[4,2,4,256,256]{4,3,2,1,0:T(8,128)} %bitcast.3, s32[2,2,2,4]{3,2,1,0:T(2,128)} %codes.1, s32[512,32]{1,0:T(8,128)} %bitcast.5), custom_call_target="tpu_custom_call" | custom-call | tf_op jit(solution)/shard_map/pallas_call | solution.py:386
  59.7 1.9 %copy.8 = f32[128,8,128]{2,1,0:T(8,128)} copy(f32[128,8,128]{2,1,0:T(8,128)} %get-tuple-element.4) | data formatting | bytes 1048576
  61.5 1.5 %copy.9 = f32[128,128]{1,0:T(8,128)} copy(f32[128,128]{1,0:T(8,128)} %get-tuple-element.5) | data formatting | bytes 131072

commit v3 on v2

--- a/solution.py
+++ b/solution.py
@@ -20,6 +20,7 @@
 SLOTS = 4
 BR = 8
 BLK = 128
+CUTS = (8, 6, 12)
 
 
 def dot(a, b, dims=((1,), (0,)), precision=None):
@@ -99,7 +100,7 @@
     jv, jhi, jlo, ext0, ext1, acc, amat, omv, idxv, idxs,
     gram, rsb, part, gxb, tot, gfull, work, linv, pk, arr,
     loc_sem, jac_sem, hsend, hrecv, ar_send, ar_recv, a2a_send, a2a_recv, idx_sem,
-    far_x, farther_x, far_y,
+    far_x, farther_x, far_y, near_y,
 ):
     gx = lax.axis_index("gx")
     gy = lax.axis_index("gy")
@@ -110,23 +111,29 @@
     gy_off = lax.rem(gy + 2 * core - 1 + GY, GY)
     gy_on = lax.rem(gy + 1 - 2 * core + GY, GY)
 
-    def halo(s, src, dst, who, role):
+    def halo(s, src, dst, who, role, half=None):
+        if half is not None:
+            rows = pl.ds(half * (CELL // 2), CELL // 2)
+            src, dst = src.at[rows], dst.at[rows]
+        part_no = half or 0
         return pltpu.make_async_remote_copy(
-            src_ref=src, dst_ref=dst, send_sem=hsend.at[s, role], recv_sem=hrecv.at[s, role],
-            device_id=who, device_id_type=MESH,
+            src_ref=src, dst_ref=dst, send_sem=hsend.at[s, role, part_no],
+            recv_sem=hrecv.at[s, role, part_no], device_id=who, device_id_type=MESH,
         )
 
     def own(s, ext, a, b):
         return tan.at[a * 2 + b] if s == 0 else ext.at[(1 + a) * 4 + 1 + b]
 
     def own_copies(s, ext):
-        cols = (off, on)
-        x_copies = [
-            (
-                halo(s, own(s, ext, 1, cols[k]), ext.at[1 + cols[k]], (gx_hi, gy), k),
-                halo(s, own(s, ext, 0, cols[k]), ext.at[12 + 1 + cols[k]], (gx_lo, gy), 2 + k),
-            )
-            for k in range(2)
+        x_off, x_on = [
+            [
+                (
+                    halo(s, own(s, ext, 1, col), ext.at[1 + col], (gx_hi, gy), k, half),
+                    halo(s, own(s, ext, 0, col), ext.at[12 + 1 + col], (gx_lo, gy), 2 + k, half),
+                )
+                for half in halves
+            ]
+            for k, col, halves in ((0, off, (0, 1)), (1, on, (None,)))
         ]
         y_off = [
             halo(s, own(s, ext, a, off), ext.at[(1 + a) * 4 + 3 * on], (gx, gy_off), 4 + a)
@@ -136,12 +143,18 @@
             halo(s, own(s, ext, a, on), ext.at[(1 + a) * 4 + 3 * off], (gx, gy_on), 6 + a)
             for a in range(2)
         ]
-        return x_copies, y_off, y_on
+        return x_off, x_on, y_off, y_on
 
     def corner_copies(s, ext):
         c_off = [
-            halo(s, ext.at[12 * side + 1 + off], ext.at[12 * side + 3 * on], (gx, gy_off), 8 + side)
-            for side in range(2)
+            [
+                halo(
+                    s, ext.at[12 * side + 1 + off], ext.at[12 * side + 3 * on], (gx, gy_off),
+                    8 + side, half,
+                )
+                for side in range(2)
+            ]
+            for half in range(2)
         ]
         c_on = [
             halo(s, ext.at[12 * side + 1 + on], ext.at[12 * side + 3 * off], (gx, gy_on), 10 + side)
@@ -176,8 +189,8 @@
         copy.start()
     pl.semaphore_wait(barrier, 4)
 
-    x_c, y_off, y_on = own_copies(0, ext0)
-    for copy in (*x_c[0], *y_off, *x_c[1], *y_on):
+    x_off, x_on, y_off, y_on = own_copies(0, ext0)
+    for copy in (*x_off[0], *x_off[1], *y_off, *x_on[0], *y_on):
         copy.start()
 
     def product(s, cell, slot, field):
@@ -240,7 +253,7 @@
     idx_copy = None
     for s in range(SWEEPS):
         ext = exts[s]
-        sent += [*x_c[0], *x_c[1], *y_off, *y_on]
+        sent += [*x_off[0], *x_off[1], *x_on[0], *y_off, *y_on]
         if s == 0:
             jac_copies[0].wait()
             split_jacobians(0)
@@ -248,11 +261,12 @@
                 copy.wait()
         own_terms(s, ext)
         c_off, c_on = corner_copies(s, ext)
-        for copy in x_c[0]:
-            copy.wait_recv()
-        for copy in c_off:
-            copy.start()
-        for copy in x_c[1]:
+        for half in range(2):
+            for copy in x_off[half]:
+                copy.wait_recv()
+            for copy in c_off[half]:
+                copy.start()
+        for copy in x_on[0]:
             copy.wait_recv()
         for copy in c_on:
             copy.start()
@@ -260,13 +274,14 @@
             greet(far_x, (along_x(2), along_x(-2)))
         else:
             pl.semaphore_wait(farther_x, 2)
-        sent += [*c_off, *c_on]
+            greet(near_y, (along_y(1), along_y(-1)))
+        sent += [*c_off[0], *c_off[1], *c_on]
         if s == 0:
             jac_copies[1].wait()
             split_jacobians(1)
             own_copy.wait()
             idx_copy = routing()
-        for copy in (*y_on, *y_off, *c_on, *c_off):
+        for copy in (*y_on, *y_off, *c_on, *c_off[0], *c_off[1]):
             copy.wait_recv()
         if s == 0:
             pl.semaphore_wait(far_x, 2)
@@ -274,9 +289,10 @@
             greet(far_y, (along_y(2), along_y(-2)))
         else:
             pl.semaphore_wait(far_y, 2)
+            pl.semaphore_wait(near_y, 2)
 
         if s == 0:
-            x_c, y_off, y_on = own_copies(1, ext1)
+            x_off, x_on, y_off, y_on = own_copies(1, ext1)
         for n in range(4):
             a, b = n % 2, (off if n < 2 else on)
             cell = a * 2 + b
@@ -292,10 +308,10 @@
             if s == 0:
                 ext1[(1 + a) * 4 + 1 + b] = total
                 if n == 1:
-                    for copy in (*x_c[0], *y_off):
+                    for copy in (*x_off[0], *x_off[1], *y_off):
                         copy.start()
                 if n == 3:
-                    for copy in (*x_c[1], *y_on):
+                    for copy in (*x_on[0], *y_on):
                         copy.start()
             else:
                 amat[pl.ds(cell * 32, 32)] = total.reshape(32, BR, VEC)
@@ -325,16 +341,26 @@
         pk[o, 1] = amat[idxs[1, o] & (BLK - 1)]
         return carry
 
-    def send(step, carry):
-        o = lax.rem(me + 37 * step, TILES)
-        pltpu.make_async_remote_copy(
-            src_ref=pk.at[o], dst_ref=arr.at[me], send_sem=a2a_send, recv_sem=a2a_recv,
-            device_id=(lax.div(o, GY), lax.rem(o, GY)), device_id_type=MESH,
-        ).start()
-        return carry
+    near, away = (0, 1, GY - 1), tuple(range(2, GY - 1))
+
+    def send(places):
+        def body(turn, carry):
+            to_x = (gx + 7 * turn) & (GX - 1)
+            for step in places:
+                to_y = (gy + step) & (GY - 1)
+                pltpu.make_async_remote_copy(
+                    src_ref=pk.at[to_x * GY + to_y], dst_ref=arr.at[me],
+                    send_sem=a2a_send, recv_sem=a2a_recv,
+                    device_id=(to_x, to_y), device_id_type=MESH,
+                ).start()
+            return carry
+
+        return body
 
     lax.fori_loop(0, TILES, pack, 0, unroll=8)
     arr[me] = pk[me]
+    send(near[1:])(0, 0)
+    lax.fori_loop(1, CUTS[0], send(near), 0)
     wait_bytes(rsb.at[pl.ds(0, GY - 1)], ar_recv.at[0])
     mine = jnp.sum(rsb[...], axis=0)
     part[...] = mine
@@ -344,16 +370,17 @@
             device_id=(lax.rem(gx + step, GX), gy), device_id_type=MESH,
         ).start()
     gxb[gx] = mine
-    lax.fori_loop(1, 49, send, 0)
+    lax.fori_loop(CUTS[0], GX, send(near), 0)
+    lax.fori_loop(0, CUTS[1], send(away), 0)
     wait_bytes(gxb.at[pl.ds(0, GX - 1)], ar_recv.at[1])
     mine = jnp.sum(gxb[...], axis=0) * (1.0 / ROWS)
     tot[...] = mine
     for step in range(1, GY):
         to_gy(step, lambda k: tot, gfull.at[pl.ds(gy * share, share)], 2).start()
     gfull[pl.ds(gy * share, share), :] = mine
-    lax.fori_loop(49, 97, send, 0)
+    lax.fori_loop(CUTS[1], CUTS[2], send(away), 0)
     wait_bytes(gfull.at[pl.ds(0, (GY - 1) * share)], ar_recv.at[2])
-    lax.fori_loop(97, TILES, send, 0)
+    lax.fori_loop(CUTS[2], GX, send(away), 0)
 
     eye = (iota((VEC, VEC), 0) == iota((VEC, VEC), 1)).astype(F32)
     work[:, :VEC] = gfull[...]
@@ -414,13 +441,14 @@
             pltpu.VMEM((TILES, 2, BR, VEC), F32),
             pltpu.SemaphoreType.DMA((5,)),
             pltpu.SemaphoreType.DMA((SWEEPS,)),
-            pltpu.SemaphoreType.DMA((SWEEPS, 12)),
-            pltpu.SemaphoreType.DMA((SWEEPS, 12)),
+            pltpu.SemaphoreType.DMA((SWEEPS, 12, 2)),
+            pltpu.SemaphoreType.DMA((SWEEPS, 12, 2)),
             pltpu.SemaphoreType.DMA((3,)),
             pltpu.SemaphoreType.DMA((3,)),
             pltpu.SemaphoreType.DMA,
             pltpu.SemaphoreType.DMA,
             pltpu.SemaphoreType.DMA,
+            pltpu.SemaphoreType.REGULAR,
             pltpu.SemaphoreType.REGULAR,
             pltpu.SemaphoreType.REGULAR,
             pltpu.SemaphoreType.REGULAR,

time: 63.2 us -> 62.3 us (0.986)
  Pallas kernels: 59 us -> 58.1 us
    pallas_call x1, Pallas kernels: 59 us -> 58.1 us  [shards(): pl.pallas_call(kernel, out_shape=(jax.ShapeDtypeStruct((BLK, BR, VEC), F3...]
where the time goes in v3:
time: 62.3 us; the launch traced here: 62.1 us
  Pallas kernels  58.1 us (93%)
  local copies, waits for them, and re-layouts  3.34 us (5%)
  between operations  0.64 us (1%)
    pallas_call x1, Pallas kernels, shards(): pl.pallas_call(kernel, out_shape=(jax.ShapeDtypeStruct((BLK, BR, VEC), F3...  58.1 us
    unnamed x2, local copies, waits for them, and re-layouts  3.34 us

profile of v3, /device:TPU:1, one launch (start us, length us, event | category | flops | bytes accessed | tf_op | source)
XLA Modules:
  0.0 62.1 jit_solution(28088785831285680)
XLA Ops:
  0.6 58.1 %shard_map.59 = (f32[128,8,128]{2,1,0:T(8,128)}, f32[128,128]{1,0:T(8,128)}) custom-call(f32[4,256,128]{2,1,0:T(8,128)} %bitcast.4, f32[4,2,4,256,256]{4,3,2,1,0:T(8,128)} %bitcast.3, s32[2,2,2,4]{3,2,1,0:T(2,128)} %codes.1, s32[512,32]{1,0:T(8,128)} %bitcast.5), custom_call_target="tpu_custom_call" | custom-call | tf_op jit(solution)/shard_map/pallas_call | solution.py:413
  58.7 1.9 %copy.8 = f32[128,8,128]{2,1,0:T(8,128)} copy(f32[128,8,128]{2,1,0:T(8,128)} %get-tuple-element.4) | data formatting | bytes 1048576
  60.6 1.5 %copy.9 = f32[128,128]{1,0:T(8,128)} copy(f32[128,128]{1,0:T(8,128)} %get-tuple-element.5) | data formatting | bytes 131072

commit v4 on v3

--- a/solution.py
+++ b/solution.py
@@ -20,7 +20,7 @@
 SLOTS = 4
 BR = 8
 BLK = 128
-CUTS = (8, 6, 12)
+CUTS = (12, 5, 12)
 
 
 def dot(a, b, dims=((1,), (0,)), precision=None):
@@ -98,7 +98,7 @@
 def kernel(
     tan, jac, codes, owners, q_out, r_out,
     jv, jhi, jlo, ext0, ext1, acc, amat, omv, idxv, idxs,
-    gram, rsb, part, gxb, tot, gfull, work, linv, pk, arr,
+    gram, rsb, part, gyb, tot, gfull, work, linv, pk, arr,
     loc_sem, jac_sem, hsend, hrecv, ar_send, ar_recv, a2a_send, a2a_recv, idx_sem,
     far_x, farther_x, far_y, near_y,
 ):
@@ -318,21 +318,21 @@
 
     rows_all = amat[...].reshape(4 * CELL, VEC)
     gram[...] = dot(rows_all, rows_all, ((0,), (0,)), FULL)
-    share = VEC // GY
-
-    def to_gy(step, src, dst, phase):
-        k = lax.rem(gy + step, GY)
+    share = VEC // GX
+
+    def to_gx(step, src, dst, phase):
+        k = lax.rem(gx + step, GX)
         return pltpu.make_async_remote_copy(
             src_ref=src(k), dst_ref=dst, send_sem=ar_send.at[phase], recv_sem=ar_recv.at[phase],
-            device_id=(gx, k), device_id_type=MESH,
+            device_id=(k, gy), device_id_type=MESH,
         )
 
     def wait_bytes(ref, sem):
         pltpu.make_async_copy(ref, ref, sem).wait()
 
-    for step in range(1, GY):
-        to_gy(step, lambda k: gram.at[pl.ds(k * share, share)], rsb.at[gy], 0).start()
-    rsb[gy] = gram[pl.ds(gy * share, share), :]
+    for step in range(1, GX):
+        to_gx(step, lambda k: gram.at[pl.ds(k * share, share)], rsb.at[gx], 0).start()
+    rsb[gx] = gram[pl.ds(gx * share, share), :]
 
     idx_copy.wait()
 
@@ -361,25 +361,25 @@
     arr[me] = pk[me]
     send(near[1:])(0, 0)
     lax.fori_loop(1, CUTS[0], send(near), 0)
-    wait_bytes(rsb.at[pl.ds(0, GY - 1)], ar_recv.at[0])
+    wait_bytes(rsb.at[pl.ds(0, GX - 1)], ar_recv.at[0])
     mine = jnp.sum(rsb[...], axis=0)
     part[...] = mine
-    for step in range(1, GX):
+    for step in range(1, GY):
         pltpu.make_async_remote_copy(
-            src_ref=part, dst_ref=gxb.at[gx], send_sem=ar_send.at[1], recv_sem=ar_recv.at[1],
-            device_id=(lax.rem(gx + step, GX), gy), device_id_type=MESH,
+            src_ref=part, dst_ref=gyb.at[gy], send_sem=ar_send.at[1], recv_sem=ar_recv.at[1],
+            device_id=(gx, lax.rem(gy + step, GY)), device_id_type=MESH,
         ).start()
-    gxb[gx] = mine
+    gyb[gy] = mine
     lax.fori_loop(CUTS[0], GX, send(near), 0)
     lax.fori_loop(0, CUTS[1], send(away), 0)
-    wait_bytes(gxb.at[pl.ds(0, GX - 1)], ar_recv.at[1])
-    mine = jnp.sum(gxb[...], axis=0) * (1.0 / ROWS)
+    wait_bytes(gyb.at[pl.ds(0, GY - 1)], ar_recv.at[1])
+    mine = jnp.sum(gyb[...], axis=0) * (1.0 / ROWS)
     tot[...] = mine
-    for step in range(1, GY):
-        to_gy(step, lambda k: tot, gfull.at[pl.ds(gy * share, share)], 2).start()
-    gfull[pl.ds(gy * share, share), :] = mine
+    for step in range(1, GX):
+        to_gx(step, lambda k: tot, gfull.at[pl.ds(gx * share, share)], 2).start()
+    gfull[pl.ds(gx * share, share), :] = mine
     lax.fori_loop(CUTS[1], CUTS[2], send(away), 0)
-    wait_bytes(gfull.at[pl.ds(0, (GY - 1) * share)], ar_recv.at[2])
+    wait_bytes(gfull.at[pl.ds(0, (GX - 1) * share)], ar_recv.at[2])
     lax.fori_loop(CUTS[2], GX, send(away), 0)
 
     eye = (iota((VEC, VEC), 0) == iota((VEC, VEC), 1)).astype(F32)
@@ -400,9 +400,9 @@
 
     for copy in sent:
         copy.wait_send()
-    wait_bytes(rsb.at[pl.ds(0, GY - 1)], ar_send.at[0])
-    wait_bytes(gxb.at[pl.ds(0, GX - 1)], ar_send.at[1])
-    wait_bytes(gfull.at[pl.ds(0, (GY - 1) * share)], ar_send.at[2])
+    wait_bytes(rsb.at[pl.ds(0, GX - 1)], ar_send.at[0])
+    wait_bytes(gyb.at[pl.ds(0, GY - 1)], ar_send.at[1])
+    wait_bytes(gfull.at[pl.ds(0, (GX - 1) * share)], ar_send.at[2])
     wait_bytes(arr.at[pl.ds(0, TILES - 1)], a2a_send)
 
 
@@ -430,10 +430,10 @@
             pltpu.VMEM((8, VEC), I32),
             pltpu.SMEM((8, VEC), I32),
             pltpu.VMEM((VEC, VEC), F32),
-            pltpu.VMEM((GY, VEC // GY, VEC), F32),
-            pltpu.VMEM((VEC // GY, VEC), F32),
-            pltpu.VMEM((GX, VEC // GY, VEC), F32),
-            pltpu.VMEM((VEC // GY, VEC), F32),
+            pltpu.VMEM((GX, VEC // GX, VEC), F32),
+            pltpu.VMEM((VEC // GX, VEC), F32),
+            pltpu.VMEM((GY, VEC // GX, VEC), F32),
+            pltpu.VMEM((VEC // GX, VEC), F32),
             pltpu.VMEM((VEC, VEC), F32),
             pltpu.VMEM((VEC, 2 * VEC), F32),
             pltpu.VMEM((VEC, VEC), F32),

time: 62.3 us -> 59.5 us (0.955)
  Pallas kernels: 58.1 us -> 55.3 us
    pallas_call x1, Pallas kernels: 58.1 us -> 55.3 us  [shards(): pl.pallas_call(kernel, out_shape=(jax.ShapeDtypeStruct((BLK, BR, VEC), F3...]
where the time goes in v4:
time: 59.5 us; the launch traced here: 59.3 us
  Pallas kernels  55.3 us (93%)
  local copies, waits for them, and re-layouts  3.34 us (6%)
  between operations  0.64 us (1%)
    pallas_call x1, Pallas kernels, shards(): pl.pallas_call(kernel, out_shape=(jax.ShapeDtypeStruct((BLK, BR, VEC), F3...  55.3 us
    unnamed x2, local copies, waits for them, and re-layouts  3.34 us

profile of v4, /device:TPU:1, one launch (start us, length us, event | category | flops | bytes accessed | tf_op | source)
XLA Modules:
  0.0 59.3 jit_solution(11065431448605099702)
XLA Ops:
  0.6 55.3 %shard_map.59 = (f32[128,8,128]{2,1,0:T(8,128)}, f32[128,128]{1,0:T(8,128)}) custom-call(f32[4,256,128]{2,1,0:T(8,128)} %bitcast.4, f32[4,2,4,256,256]{4,3,2,1,0:T(8,128)} %bitcast.3, s32[2,2,2,4]{3,2,1,0:T(2,128)} %codes.1, s32[512,32]{1,0:T(8,128)} %bitcast.5), custom_call_target="tpu_custom_call" | custom-call | tf_op jit(solution)/shard_map/pallas_call | solution.py:413
  56.0 1.9 %copy.8 = f32[128,8,128]{2,1,0:T(8,128)} copy(f32[128,8,128]{2,1,0:T(8,128)} %get-tuple-element.4) | data formatting | bytes 1048576
  57.8 1.5 %copy.9 = f32[128,128]{1,0:T(8,128)} copy(f32[128,128]{1,0:T(8,128)} %get-tuple-element.5) | data formatting | bytes 131072

commit v5 on v4

--- a/solution.py
+++ b/solution.py
@@ -66,7 +66,6 @@
     for j in range(BR):
         pivot = block[j][j]
         inv = lax.rsqrt(pivot)
-        inv = inv * (1.5 - 0.5 * (pivot * inv) * inv)
         rows_l[j] = rows_l[j] * inv
         rows_r[j] = rows_r[j] * inv
         below = [block[i][j] * inv if i > j else None for i in range(BR)]

time: 59.5 us -> 59 us (level)
  no operation moved by 1% of the time
where the time goes in v5:
time: 59 us; the launch traced here: 58.8 us
  Pallas kernels  54.8 us (93%)
  local copies, waits for them, and re-layouts  3.34 us (6%)
  between operations  0.64 us (1%)
    pallas_call x1, Pallas kernels, shards(): pl.pallas_call(kernel, out_shape=(jax.ShapeDtypeStruct((BLK, BR, VEC), F3...  54.8 us
    unnamed x2, local copies, waits for them, and re-layouts  3.34 us

profile of v5, /device:TPU:1, one launch (start us, length us, event | category | flops | bytes accessed | tf_op | source)
XLA Modules:
  0.0 58.8 jit_solution(8322584179100225143)
XLA Ops:
  0.6 54.8 %shard_map.59 = (f32[128,8,128]{2,1,0:T(8,128)}, f32[128,128]{1,0:T(8,128)}) custom-call(f32[4,256,128]{2,1,0:T(8,128)} %bitcast.4, f32[4,2,4,256,256]{4,3,2,1,0:T(8,128)} %bitcast.3, s32[2,2,2,4]{3,2,1,0:T(2,128)} %codes.1, s32[512,32]{1,0:T(8,128)} %bitcast.5), custom_call_target="tpu_custom_call" | custom-call | tf_op jit(solution)/shard_map/pallas_call | solution.py:412
  55.5 1.9 %copy.8 = f32[128,8,128]{2,1,0:T(8,128)} copy(f32[128,8,128]{2,1,0:T(8,128)} %get-tuple-element.4) | data formatting | bytes 1048576
  57.3 1.5 %copy.9 = f32[128,128]{1,0:T(8,128)} copy(f32[128,128]{1,0:T(8,128)} %get-tuple-element.5) | data formatting | bytes 131072
